TPU v7x, 512 devices: a whole 4x8x8 slice. The times are simulated.
512 devices in a mesh: shot: 16 (over y, z_lo), seq: 32 (over z_hi, x, core).
Axes of the slice: x: 4, y: 8, z: 8 (z_hi: 4, z_lo: 2; z = z_hi * 2 + z_lo), core: 2. Of those that a mesh axis runs over, the one named last changes fastest.
Arguments:
- queries: bfloat16 [16, 4096, 1536], P('shot', 'seq'), may hold values from -120 to 120
- key_rows: bfloat16 [16, 4096, 1536], P('shot', 'seq'), may hold values from -6 to 6
- values: bfloat16 [16, 4096, 1536], P('shot', 'seq'), may hold values from -6 to 6
- shot_len: int32 [16], replicated, may hold values from 128 to 4096, as said below
- anchor_len: int32 [16], replicated, may hold values from 16 to 64, as said below
- shot_group: int32 [16], replicated, may hold values from 0 to 1
Outputs:
- attended: bfloat16 [16, 4096, 1536], P('shot', 'seq')
Inputs may be any that keep to these rules, and one draw needn't show every extreme that they name: `shot_len`: each a multiple of 128; in every draw some shot has all 4096 slots live. `anchor_len`: in every draw some shot has 64 anchor tokens.
All inputs are finite; a program needn't handle non-finite values.
Results may differ from a plain program's by a relative error of at most 0.0036.
Values may be sent and summed in bfloat16 or wider, within the bound.
A program may use at most 64 MiB of HBM per device.

v0:
```python
import math

import jax
import jax.numpy as jnp
from jax import lax
from jax.sharding import PartitionSpec as P

HEADS = 12
HDIM = 128
ANCH = 64


def from_behind(block, axis, distance):
    devices = range(lax.axis_size(axis))
    route = [((i - distance) % len(devices), i) for i in devices]
    return lax.ppermute(block, axis, route)


def attend(query, own_keys, own_vals, own_live, far_keys, far_vals, far_live, own_count, own_block):
    score_scale = 1.0 / math.sqrt(query.shape[1])
    row_count = query.shape[0]
    query_block = math.gcd(row_count, 256)
    shot_cap = own_keys.shape[0]

    def one_rows(block_index):
        query_piece = lax.dynamic_slice_in_dim(query, block_index * query_block, query_block, 0)

        def fill(key_index, buffer):
            first_row = key_index * own_block
            key_piece = lax.dynamic_slice_in_dim(own_keys, first_row, own_block, 0)
            live_piece = lax.dynamic_slice_in_dim(own_live, first_row, own_block, 0)
            found = (
                lax.dot_general(
                    query_piece,
                    key_piece,
                    (((1,), (1,)), ((), ())),
                    preferred_element_type=jnp.float32,
                )
                * score_scale
            )
            found = jnp.where(live_piece[None, :], found, -jnp.inf)
            return lax.dynamic_update_slice_in_dim(buffer, found, first_row, 1)

        own_scores = lax.fori_loop(
            0, own_count, fill, jnp.full((query_block, shot_cap), -jnp.inf, jnp.float32)
        )
        far_scores = (
            lax.dot_general(
                query_piece, far_keys, (((1,), (1,)), ((), ())), preferred_element_type=jnp.float32
            )
            * score_scale
        )
        far_scores = jnp.where(far_live[None, :], far_scores, -jnp.inf)
        row_best = jnp.maximum(jnp.max(own_scores, axis=1), jnp.max(far_scores, axis=1))
        own_expo = jnp.exp(own_scores - row_best[:, None])
        far_expo = jnp.exp(far_scores - row_best[:, None])
        row_total = jnp.sum(own_expo, axis=1) + jnp.sum(far_expo, axis=1)
        own_weights = own_expo.astype(jnp.bfloat16)

        def add(key_index, summed):
            first_row = key_index * own_block
            weight_piece = lax.dynamic_slice_in_dim(own_weights, first_row, own_block, 1)
            val_piece = lax.dynamic_slice_in_dim(own_vals, first_row, own_block, 0)
            return summed + jnp.dot(weight_piece, val_piece, preferred_element_type=jnp.float32)

        start_sum = jnp.dot(
            far_expo.astype(jnp.bfloat16), far_vals, preferred_element_type=jnp.float32
        )
        summed = lax.fori_loop(0, own_count, add, start_sum)
        return summed / row_total[:, None]

    blocks = lax.map(one_rows, jnp.arange(row_count // query_block, dtype=jnp.int32))
    return blocks.reshape(row_count, query.shape[1])


def local(queries, key_rows, values, shot_len, anchor_len, shot_group):
    seq_count = lax.axis_size("seq")
    groups = math.gcd(HEADS, seq_count)
    parts_per = seq_count // groups
    tok_rows = queries.shape[1]
    sub_rows = tok_rows // parts_per
    col_width = queries.shape[2] // groups
    shot_cap = tok_rows * seq_count
    seq_place = lax.axis_index("seq")
    shot_here = lax.axis_index("shot")
    my_part = seq_place // groups

    def split_rows(source):
        return (
            source.reshape(parts_per, sub_rows, groups, col_width)
            .transpose(0, 2, 1, 3)
            .reshape(seq_count, sub_rows, col_width)
        )

    taken_query, taken_keys, taken_vals = (
        lax.all_to_all(split_rows(queries), "seq", split_axis=0, concat_axis=0, tiled=True),
        lax.all_to_all(split_rows(key_rows), "seq", split_axis=0, concat_axis=0, tiled=True),
        lax.all_to_all(split_rows(values), "seq", split_axis=0, concat_axis=0, tiled=True),
    )
    moving = jnp.stack([taken_keys, taken_vals])
    carried = [moving]
    for cycle_turn in range(parts_per - 1):
        moving = from_behind(moving, "seq", groups)
        carried.append(moving)
    stacked = jnp.stack(carried[::-1])
    ordered = jnp.roll(stacked, my_part + 1, axis=0)
    joined = ordered.transpose(1, 2, 0, 3, 4).reshape(2, shot_cap, col_width)
    shot_keys = joined[0]
    shot_vals = joined[1]
    anchor_pair = jnp.stack([shot_keys[:ANCH], shot_vals[:ANCH]])
    anchor_all = lax.all_gather(anchor_pair, "shot", axis=1, tiled=True)
    shot_total = anchor_len.shape[0]
    anchor_ids = jnp.arange(ANCH, dtype=jnp.int32)
    shot_ids = jnp.arange(shot_total, dtype=jnp.int32)
    reach = (
        (anchor_ids[None, :] < anchor_len[:, None])
        & (shot_group == shot_group[shot_here])[:, None]
        & (shot_ids != shot_here)[:, None]
    )
    anchor_live = reach.reshape(shot_total * ANCH)
    own_live = jnp.arange(shot_cap, dtype=jnp.int32) < shot_len[shot_here]
    query_pos = (
        jnp.arange(seq_count, dtype=jnp.int32)[:, None] * tok_rows
        + my_part * sub_rows
        + jnp.arange(sub_rows, dtype=jnp.int32)[None, :]
    )
    query_live = query_pos.reshape(seq_count * sub_rows) < shot_len[shot_here]
    own_block = math.gcd(shot_cap, 2048)
    own_count = shot_cap // own_block
    flat_query = taken_query.reshape(seq_count * sub_rows, col_width)
    results = []
    for head_index in range(col_width // HDIM):
        head_start = head_index * HDIM
        head_stop = head_start + HDIM
        results.append(
            attend(
                flat_query[:, head_start:head_stop],
                shot_keys[:, head_start:head_stop],
                shot_vals[:, head_start:head_stop],
                own_live,
                anchor_all[0][:, head_start:head_stop],
                anchor_all[1][:, head_start:head_stop],
                anchor_live,
                own_count,
                own_block,
            )
        )
    blended = jnp.concatenate(results, axis=1)
    finished = (
        jnp.where(query_live[:, None], blended, 0.0)
        .astype(jnp.bfloat16)
        .reshape(seq_count, sub_rows, col_width)
    )
    returned = lax.all_to_all(finished, "seq", split_axis=0, concat_axis=0, tiled=True)
    return (
        returned.reshape(parts_per, groups, sub_rows, col_width)
        .transpose(0, 2, 1, 3)
        .reshape(1, tok_rows, groups * col_width)
    )


def solution(mesh):
    in_specs = (
        P("shot", "seq", None),
        P("shot", "seq", None),
        P("shot", "seq", None),
        P(),
        P(),
        P(),
    )
    out_specs = P("shot", "seq", None)
    return jax.shard_map(local, mesh=mesh, in_specs=in_specs, out_specs=out_specs, check_vma=False)
```

profile of v0, /device:TPU:1, one launch (start us, length us, event | category | flops | bytes accessed | tf_op | source)
XLA Modules:
  0.0 633.8 jit_solution(12750380868871086092)
XLA Ops:
  8.4 14.4 %all-to-all-start.2 = ((bf16[32,16,384]{2,1,0:T(8,128)(2,1)}), bf16[32,16,384]{2,1,0:T(8,128)(2,1)S(1)}, u32[]{:S(2)}, u32[]{:S(2)}) async-start(bf16[32,16,384]{2,1,0:T(8,128)(2,1)} %bitcast.11), calls=%async_computation.2 | async-start | bytes 786432 | tf_op jit(solution)/shard_map/all_to_all | solution.py:98
  24.1 14.3 %all-to-all-done.2 = bf16[32,16,384]{2,1,0:T(8,128)(2,1)S(1)} async-done(((bf16[32,16,384]{2,1,0:T(8,128)(2,1)}), bf16[32,16,384]{2,1,0:T(8,128)(2,1)S(1)}, u32[]{:S(2)}, u32[]{:S(2)}) %all-to-all-start.2) | async-done | bytes 393248 | tf_op jit(solution)/shard_map/all_to_all | solution.py:98
  38.4 20.1 %all_to_all.20 = bf16[32,16,384]{2,1,0:T(8,128)(2,1)S(1)} all-to-all(bf16[32,16,384]{2,1,0:T(8,128)(2,1)S(1)} %bitcast.161), channel_id=1, replica_groups=mesh['shot'=16,'seq'=32] {'seq'}, dimensions={0} | all-to-all | bytes 786432 | tf_op jit(solution)/shard_map/all_to_all | solution.py:97
  58.6 2.5 collective-permute-start
  61.1 39.9 %collective-permute-done = bf16[2,32,16,384]{3,2,1,0:T(8,128)(2,1)S(1)} collective-permute-done((bf16[2,32,16,384]{3,2,1,0:T(8,128)(2,1)S(1)}, bf16[2,32,16,384]{3,2,1,0:T(8,128)(2,1)S(1)}, u32[]{:S(2)}, u32[]{:S(2)}) %collective-permute-start) | collective-permute-done | bytes 786464 | tf_op jit(solution)/shard_map/ppermute | solution.py:16
  102.9 32.7 %collective-permute-done.1 = bf16[2,32,16,384]{3,2,1,0:T(8,128)(2,1)S(1)} collective-permute-done((bf16[2,32,16,384]{3,2,1,0:T(8,128)(2,1)S(1)}, bf16[2,32,16,384]{3,2,1,0:T(8,128)(2,1)S(1)}, u32[]{:S(2)}, u32[]{:S(2)}) %collective-permute-start.1) | collective-permute-done | bytes 786464 | tf_op jit(solution)/shard_map/ppermute | solution.py:16
  137.5 18.1 %collective-permute-done.2 = bf16[2,32,16,384]{3,2,1,0:T(8,128)(2,1)S(1)} collective-permute-done((bf16[2,32,16,384]{3,2,1,0:T(8,128)(2,1)S(1)}, bf16[2,32,16,384]{3,2,1,0:T(8,128)(2,1)S(1)}, u32[]{:S(2)}, u32[]{:S(2)}) %collective-permute-start.2) | collective-permute-done | bytes 786464 | tf_op jit(solution)/shard_map/ppermute | solution.py:16
  157.5 29.1 %collective-permute-done.3 = bf16[2,32,16,384]{3,2,1,0:T(8,128)(2,1)S(1)} collective-permute-done((bf16[2,32,16,384]{3,2,1,0:T(8,128)(2,1)S(1)}, bf16[2,32,16,384]{3,2,1,0:T(8,128)(2,1)S(1)}, u32[]{:S(2)}, u32[]{:S(2)}) %collective-permute-start.3) | collective-permute-done | bytes 786464 | tf_op jit(solution)/shard_map/ppermute | solution.py:16
  189.4 33.8 %collective-permute-done.4 = bf16[2,32,16,384]{3,2,1,0:T(8,128)(2,1)S(1)} collective-permute-done((bf16[2,32,16,384]{3,2,1,0:T(8,128)(2,1)S(1)}, bf16[2,32,16,384]{3,2,1,0:T(8,128)(2,1)S(1)}, u32[]{:S(2)}, u32[]{:S(2)}) %collective-permute-start.4) | collective-permute-done | bytes 786464 | tf_op jit(solution)/shard_map/ppermute | solution.py:16
  226.1 31.8 %collective-permute-done.5 = bf16[2,32,16,384]{3,2,1,0:T(8,128)(2,1)} collective-permute-done((bf16[2,32,16,384]{3,2,1,0:T(8,128)(2,1)S(1)}, bf16[2,32,16,384]{3,2,1,0:T(8,128)(2,1)}, u32[]{:S(2)}, u32[]{:S(2)}) %collective-permute-start.5) | collective-permute-done | bytes 786464 | tf_op jit(solution)/shard_map/ppermute | solution.py:16
  259.8 33.1 %collective-permute-done.6 = bf16[2,32,16,384]{3,2,1,0:T(8,128)(2,1)} collective-permute-done((bf16[2,32,16,384]{3,2,1,0:T(8,128)(2,1)}, bf16[2,32,16,384]{3,2,1,0:T(8,128)(2,1)}, u32[]{:S(2)}, u32[]{:S(2)}) %collective-permute-start.6) | collective-permute-done | bytes 786464 | tf_op jit(solution)/shard_map/ppermute | solution.py:16
  292.9 2.1 bitcast_dynamic-update-slice_fusion.15
  295.0 2.2 bitcast_dynamic-update-slice_fusion.13
  304.4 2.2 bitcast_dynamic-update-slice_fusion.16
  306.6 2.2 bitcast_dynamic-update-slice_fusion.14
  314.9 3.4 dynamic-slice_bitcast_fusion
  323.3 30.6 %all-to-all-start = ((bf16[32,16,384]{2,1,0:T(8,128)(2,1)}), bf16[32,16,384]{2,1,0:T(8,128)(2,1)S(1)}, u32[]{:S(2)}, u32[]{:S(2)}) async-start(bf16[32,16,384]{2,1,0:T(8,128)(2,1)} %bitcast.160), calls=%async_computation | async-start | bytes 786432 | tf_op jit(solution)/shard_map/all_to_all | solution.py:96
  357.2 10.9 %all-to-all-done = bf16[32,16,384]{2,1,0:T(8,128)(2,1)S(1)} async-done(((bf16[32,16,384]{2,1,0:T(8,128)(2,1)}), bf16[32,16,384]{2,1,0:T(8,128)(2,1)S(1)}, u32[]{:S(2)}, u32[]{:S(2)}) %all-to-all-start) | async-done | bytes 393248 | tf_op jit(solution)/shard_map/all_to_all | solution.py:96
  368.9 4.6 fusion.71
  373.5 48.6 %all-gather.2.cloned.1.call-done = bf16[2,1024,384]{2,1,0:T(8,128)(2,1)} async-done(((bf16[2,64,384]{2,1,0:T(8,128)(2,1)}), bf16[2,1024,384]{2,1,0:T(8,128)(2,1)}) %all-gather.2.cloned.1.call-update) | async-done | bytes 1572880 | tf_op jit(solution)/shard_map/all_gather | solution.py:111
  426.8 58.7 %while.119 = (s32[]{:T(128)}, bf16[2,256,128]{2,1,0:T(8,128)(2,1)}, s32[2]{0:T(128)}, bf16[512,128]{1,0:T(8,128)(2,1)}, bf16[1024,128]{1,0:T(8,128)(2,1)}, /*ind...) while((s32[]{:T(128)}, bf16[2,256,128]{2,1,0:T(8,128)(2,1)}, ...), condition=%wide.region_9.10_spmd.clone, body=%wide.region_0.9_spmd.clone.sunk | while | flops 409803264 | bytes 33983396 | solution.py:72
  430.2 2.2 broadcast.106
  432.4 5.7 while.126
  432.4 2.8 fusion.169
  435.3 2.8 fusion.169
  438.1 2.7 reduce_max.70
  442.3 5.7 copy.71
  448.0 3.0 fusion.137
  452.3 3.0 while.127
  459.6 2.2 broadcast.106
  461.8 5.7 while.126
  461.8 2.8 fusion.169
  464.6 2.8 fusion.169
  467.4 2.7 reduce_max.70
  471.7 5.7 copy.71
  477.4 3.0 fusion.137
  481.6 3.0 while.127
  486.6 52.2 %while.122 = (s32[]{:T(128)}, bf16[2,256,128]{2,1,0:T(8,128)(2,1)}, s32[2]{0:T(128)}, bf16[512,128]{1,0:T(8,128)(2,1)}, bf16[1024,128]{1,0:T(8,128)(2,1)}, /*ind...) while((s32[]{:T(128)}, bf16[2,256,128]{2,1,0:T(8,128)(2,1)}, ...), condition=%wide.region_19.20_spmd.clone, body=%wide.region_10.19_spmd.clone.sunk | while | flops 409803264 | bytes 39226332 | solution.py:72
  490.1 2.2 broadcast.107
  492.3 3.3 while.128
  495.6 2.8 reduce_max.72
  498.9 5.7 copy.72
  504.6 3.0 fusion.146
  508.9 3.0 while.129
  516.2 2.2 broadcast.107
  518.4 3.3 while.128
  521.7 2.8 reduce_max.72
  525.0 5.7 copy.72
  530.7 3.0 fusion.146
  534.9 3.0 while.129
  539.9 51.8 %while.125 = (s32[]{:T(128)}, bf16[2,256,128]{2,1,0:T(8,128)(2,1)}, s32[2]{0:T(128)}, bf16[512,128]{1,0:T(8,128)(2,1)}, bf16[1024,128]{1,0:T(8,128)(2,1)}, /*ind...) while((s32[]{:T(128)}, bf16[2,256,128]{2,1,0:T(8,128)(2,1)}, ...), condition=%wide.region_29.30_spmd.clone, body=%wide.region_20.29_spmd.clone.sunk | while | flops 409803264 | bytes 38177728 | solution.py:72
  543.3 2.2 broadcast.108
  545.5 3.3 while.130
  548.8 2.8 reduce_max.74
  552.1 5.7 copy.73
  557.8 2.9 fusion.155
  562.0 3.0 while.131
  569.2 2.2 broadcast.108
  571.4 3.3 while.130
  574.7 2.8 reduce_max.74
  578.0 5.7 copy.73
  583.7 2.9 fusion.155
  587.9 3.0 while.131
  592.9 33.0 %all_to_all.21 = bf16[32,16,384]{2,1,0:T(8,128)(2,1)S(1)} all-to-all(bf16[32,16,384]{2,1,0:T(8,128)(2,1)S(1)} %fusion.66), channel_id=1, replica_groups=mesh['shot'=16,'seq'=32] {'seq'}, dimensions={0} | all-to-all | bytes 786432 | tf_op jit(solution)/shard_map/all_to_all | solution.py:154
  (222 shorter events, 112.8 us)
Async XLA Ops:
  8.4 29.9 %all-to-all-start.2 = ((bf16[32,16,384]{2,1,0:T(8,128)(2,1)}), bf16[32,16,384]{2,1,0:T(8,128)(2,1)S(1)}, u32[]{:S(2)}, u32[]{:S(2)}) async-start(bf16[32,16,384]{2,1,0:T(8,128)(2,1)} %bitcast.11), calls=%async_computation.2 | async-start | bytes 786432 | tf_op jit(solution)/shard_map/all_to_all | solution.py:98
  22.9 399.2 %all-gather.2.cloned.1.call-start = ((), (), s32[]{:S(2)}) async-start(), calls=%async_computation.4 | async-start | bytes 1671168 | tf_op jit(solution)/shard_map/all_gather | solution.py:111
  58.6 42.4 %collective-permute-start = (bf16[2,32,16,384]{3,2,1,0:T(8,128)(2,1)S(1)}, bf16[2,32,16,384]{3,2,1,0:T(8,128)(2,1)S(1)}, u32[]{:S(2)}, u32[]{:S(2)}) collective-permute-start(bf16[2,32,16,384]{3,2,1,0:T(8,128)(2,1)S(1)} %pad_maximum_fusion), channel_id=1, source_target_pairs={{28,0},{29,1},{30,2},{31,3},{0,4},{1,5},{2,6},{3,7},{4,8},{5,9},{6... | collective-permute-start | bytes 2359304 | tf_op jit(solution)/shard_map/ppermute | solution.py:16
  101.0 34.6 %collective-permute-start.1 = (bf16[2,32,16,384]{3,2,1,0:T(8,128)(2,1)S(1)}, bf16[2,32,16,384]{3,2,1,0:T(8,128)(2,1)S(1)}, u32[]{:S(2)}, u32[]{:S(2)}) collective-permute-start(bf16[2,32,16,384]{3,2,1,0:T(8,128)(2,1)S(1)} %collective-permute-done), channel_id=1, source_target_pairs={{28,0},{29,1},{30,2},{31,3},{0,4},{1,5},{2,6},{3,7},{4,8},{5,9},{6... | collective-permute-start | bytes 2359304 | tf_op jit(solution)/shard_map/ppermute | solution.py:16
  135.6 20.0 %collective-permute-start.2 = (bf16[2,32,16,384]{3,2,1,0:T(8,128)(2,1)S(1)}, bf16[2,32,16,384]{3,2,1,0:T(8,128)(2,1)S(1)}, u32[]{:S(2)}, u32[]{:S(2)}) collective-permute-start(bf16[2,32,16,384]{3,2,1,0:T(8,128)(2,1)S(1)} %collective-permute-done.1), channel_id=1, source_target_pairs={{28,0},{29,1},{30,2},{31,3},{0,4},{1,5},{2,6},{3,7},{4,8},{5,9},{6... | collective-permute-start | bytes 2359304 | tf_op jit(solution)/shard_map/ppermute | solution.py:16
  155.6 31.0 %collective-permute-start.3 = (bf16[2,32,16,384]{3,2,1,0:T(8,128)(2,1)S(1)}, bf16[2,32,16,384]{3,2,1,0:T(8,128)(2,1)S(1)}, u32[]{:S(2)}, u32[]{:S(2)}) collective-permute-start(bf16[2,32,16,384]{3,2,1,0:T(8,128)(2,1)S(1)} %collective-permute-done.2), channel_id=1, source_target_pairs={{28,0},{29,1},{30,2},{31,3},{0,4},{1,5},{2,6},{3,7},{4,8},{5,9},{6... | collective-permute-start | bytes 2359304 | tf_op jit(solution)/shard_map/ppermute | solution.py:16
  186.6 0.9 copy-start.7
  187.5 35.7 %collective-permute-start.4 = (bf16[2,32,16,384]{3,2,1,0:T(8,128)(2,1)S(1)}, bf16[2,32,16,384]{3,2,1,0:T(8,128)(2,1)S(1)}, u32[]{:S(2)}, u32[]{:S(2)}) collective-permute-start(bf16[2,32,16,384]{3,2,1,0:T(8,128)(2,1)S(1)} %collective-permute-done.3), channel_id=1, source_target_pairs={{28,0},{29,1},{30,2},{31,3},{0,4},{1,5},{2,6},{3,7},{4,8},{5,9},{6... | collective-permute-start | bytes 2359304 | tf_op jit(solution)/shard_map/ppermute | solution.py:16
  223.2 0.9 copy-start.9
  224.1 33.7 %collective-permute-start.5 = (bf16[2,32,16,384]{3,2,1,0:T(8,128)(2,1)S(1)}, bf16[2,32,16,384]{3,2,1,0:T(8,128)(2,1)}, u32[]{:S(2)}, u32[]{:S(2)}) collective-permute-start(bf16[2,32,16,384]{3,2,1,0:T(8,128)(2,1)S(1)} %collective-permute-done.4), channel_id=1, source_target_pairs={{28,0},{29,1},{30,2},{31,3},{0,4},{1,5},{2,6},{3,7},{4,8},{5,9},{6... | collective-permute-start | bytes 2359304 | tf_op jit(solution)/shard_map/ppermute | solution.py:16
  257.8 35.0 %collective-permute-start.6 = (bf16[2,32,16,384]{3,2,1,0:T(8,128)(2,1)}, bf16[2,32,16,384]{3,2,1,0:T(8,128)(2,1)}, u32[]{:S(2)}, u32[]{:S(2)}) collective-permute-start(bf16[2,32,16,384]{3,2,1,0:T(8,128)(2,1)} %collective-permute-done.5), channel_id=1, source_target_pairs={{28,0},{29,1},{30,2},{31,3},{0,4},{1,5},{2,6},{3,7},{4,8},{5,9},{6... | collective-permute-start | bytes 2359304 | tf_op jit(solution)/shard_map/ppermute | solution.py:16
  259.8 39.5 %copy-start.8 = (bf16[2,32,16,384]{3,2,1,0:T(8,128)(2,1)S(1)}, bf16[2,32,16,384]{3,2,1,0:T(8,128)(2,1)}, u32[]{:S(2)}) copy-start(bf16[2,32,16,384]{3,2,1,0:T(8,128)(2,1)} %copy-done.7) | copy-start | bytes 2359300
  301.3 7.4 %copy-start.10 = (bf16[2,32,16,384]{3,2,1,0:T(8,128)(2,1)S(1)}, bf16[2,32,16,384]{3,2,1,0:T(8,128)(2,1)}, u32[]{:S(2)}) copy-start(bf16[2,32,16,384]{3,2,1,0:T(8,128)(2,1)} %copy-done.9) | copy-start | bytes 2359300
  318.4 35.5 %copy-start.21 = (s32[16]{0:T(128)S(1)}, s32[16]{0:T(128)}, u32[]{:S(2)}) copy-start(s32[16]{0:T(128)} %param.29) | copy-start | bytes 196
  318.4 36.1 %copy-start.22 = (s32[16]{0:T(128)S(1)}, s32[16]{0:T(128)}, u32[]{:S(2)}) copy-start(s32[16]{0:T(128)} %param.27) | copy-start | bytes 196
  319.0 1.6 copy-start.2
  323.3 44.8 %all-to-all-start = ((bf16[32,16,384]{2,1,0:T(8,128)(2,1)}), bf16[32,16,384]{2,1,0:T(8,128)(2,1)S(1)}, u32[]{:S(2)}, u32[]{:S(2)}) async-start(bf16[32,16,384]{2,1,0:T(8,128)(2,1)} %bitcast.160), calls=%async_computation | async-start | bytes 786432 | tf_op jit(solution)/shard_map/all_to_all | solution.py:96
  373.5 53.2 %copy-start.17 = (s32[16]{0:T(128)S(1)}, s32[16]{0:T(128)}, u32[]{:S(2)}) copy-start(s32[16]{0:T(128)} %param.28) | copy-start | bytes 196
  448.0 3.9 copy-start.4
  452.3 3.1 copy-start.13
  452.3 3.1 copy-start.18
  455.5 0.7 copy-start.14
  477.4 3.9 copy-start.4
  481.6 3.1 copy-start.13
  481.6 3.1 copy-start.18
  484.8 0.7 copy-start.14
  486.6 5.7 copy-start.1
  495.6 3.0 copy-start.6
  504.6 3.9 copy-start.3
  508.8 3.1 copy-start.15
  508.9 3.1 copy-start.19
  512.1 0.6 copy-start.16
  512.7 5.7 copy-start.1
  521.6 3.0 copy-start.6
  530.7 3.9 copy-start.3
  534.9 3.1 copy-start.15
  534.9 3.1 copy-start.19
  538.1 0.6 copy-start.16
  539.9 5.6 copy-start
  548.8 3.0 copy-start.5
  562.0 3.1 copy-start.11
  562.0 3.1 copy-start.20
  565.2 0.7 copy-start.12
  565.8 5.6 copy-start
  574.7 3.0 copy-start.5
  587.8 3.1 copy-start.11
  587.9 3.1 copy-start.20
  591.1 0.7 copy-start.12
Sparse Core Ops, SparseCore 0:
  321.5 100.5 all-gather.1
where the time goes:
time: 637 us; the launch traced here: 634 us
  waiting for transfers between devices  292 us (46%)
  local copies, waits for them, and re-layouts  112 us (18%)
  starting transfers between devices  58.9 us (9%)
  blocking collectives  53.1 us (8%)
  other arithmetic  50.9 us (8%)
  matrix products  48.6 us (8%)
  between operations  13.7 us (2%)
    ppermute x7, waiting for transfers between devices, from_behind(): return lax.ppermute(block, axis, route)  218 us
    all_gather x1, waiting for transfers between devices, local(): anchor_all = lax.all_gather(anchor_pair, 'shot', axis=1, tiled=True)  48.6 us
    while x6, local copies, waits for them, and re-layouts, one_rows(): lax.fori_loop(0, own_count, fill, jnp.full((query_block, shot_cap), -jnp....  34.2 us
    all_to_all x1, blocking collectives, local(): lax.all_to_all(finished, 'seq', split_axis=0, concat_axis=0, tiled=True)  33 us
    all_to_all x1, starting transfers between devices, local(): lax.all_to_all(split_rows(queries), 'seq', split_axis=0, concat_axis=0, t...  30.6 us
    dot_general x12, matrix products, fill(): lax.dot_general(query_piece, key_piece, (((1,), (1,)), ((), ())), preferr...  24.4 us
    unnamed x30, local copies, waits for them, and re-layouts  23.5 us
    all_to_all x1, blocking collectives, local(): lax.all_to_all(split_rows(key_rows), 'seq', split_axis=0, concat_axis=0,...  20.1 us
  transfers between devices with their start and end apart: 10, of which 10 were waited for; matrix products, arithmetic and copies ran while one was open for 2% of the time, Pallas kernels for 0%

commit v1 on v0

v1 whole, which is shorter than its diff:
```python
import functools
import math

import jax
import jax.numpy as jnp
from jax import lax
from jax.experimental import pallas as pl
from jax.experimental.pallas import tpu as pltpu
from jax.sharding import PartitionSpec as P

MESH = pl.DeviceIdType.MESH
HEADS = 12
HDIM = 128
ANCH = 64
ROWS = 128
CHIPS = 16
SHOTS = 16
GROUP = 1024
QROWS = CHIPS * ROWS
QB = 512
DEAD = -1e30
SCALE = math.log2(math.e) / math.sqrt(HDIM)


def idle_x(zh, zl):
    return 3


def host_x(j, zh, zl):
    return lax.rem(idle_x(zh, zl) + 1 + j, 4)


def kernel(
    len_ref, anch_ref, group_ref, q_ref, k_ref, v_ref, out_ref,
    qbuf, kbuf, vbuf, obuf, sbuf, mbuf, acc,
    send_sem, q_sem, k_sem, v_sem, kf_sem, vf_sem, a_sem, asend_sem, f_sem, os_sem, o_sem,
):
    shot = lax.axis_index("shot")
    seq = lax.axis_index("seq")
    y, zl = shot // 2, shot % 2
    core, x, zh = seq % 2, (seq // 2) % 4, seq // 8
    chip = seq // 2
    place = lax.rem(x - idle_x(zh, zl) - 1 + 8, 4)
    is_host = place < 3
    head = zh * 3 + jnp.minimum(place, 2)

    vbuf[:, :, :, HDIM:] = jnp.ones((20, 2, ROWS, HDIM), jnp.bfloat16)

    sibling = (shot, chip * 2 + 1 - core)

    def mate(t):
        return (shot, t * 2 + core)

    def y_peer(k):
        return (lax.rem(y + k, 8) * 2 + zl, seq)

    partner_x = lax.rem(x - idle_x(zh, zl) + idle_x(zh, 1 - zl) + 8, 4)
    partner = (y * 2 + 1 - zl, (zh * 4 + partner_x) * 2 + core)

    barrier = pltpu.get_barrier_semaphore()

    def greet(device):
        pl.semaphore_signal(barrier, inc=1, device_id=device, device_id_type=MESH)

    lax.fori_loop(1, CHIPS, lambda i, _: (greet(mate(lax.rem(chip + i, CHIPS))), 0)[1], 0)
    lax.fori_loop(1, 8, lambda i, _: (greet(y_peer(i)), 0)[1], 0)
    greet(sibling)
    greet(partner)
    pl.semaphore_wait(barrier, CHIPS - 1 + 7 + 2)

    def remote(src, dst, ssem, rsem, device):
        return pltpu.make_async_remote_copy(
            src_ref=src, dst_ref=dst, send_sem=ssem, recv_sem=rsem,
            device_id=device, device_id_type=MESH,
        )

    def drain(ref, sem):
        pltpu.make_async_copy(ref, ref, sem).wait()

    def to_chip(src, dst, ssem, rsem, t):
        @pl.when(t == chip)
        def _():
            pltpu.make_async_copy(src, dst, rsem).start()

        @pl.when(t != chip)
        def _():
            remote(src, dst, ssem, rsem, mate(t)).start()

    def columns(h):
        return pl.ds(pl.multiple_of(h * HDIM, HDIM), HDIM)

    def anchor_at(buf, t):
        return buf.at[16 + t // 4, (t // 2) % 2, pl.ds(pl.multiple_of((t % 2) * ANCH, ANCH), ANCH), pl.ds(0, HDIM)]

    def pair_at(buf, yy):
        return buf.at[16 + yy // 2, yy % 2, :, pl.ds(0, HDIM)]

    @pl.when(seq == 0)
    def _():
        def one(h, _):
            t = (h // 3) * 4 + host_x(h % 3, h // 3, zl)
            to_chip(k_ref.at[pl.ds(0, ANCH), columns(h)], anchor_at(kbuf, shot), asend_sem.at[0], a_sem.at[0], t)
            to_chip(v_ref.at[pl.ds(0, ANCH), columns(h)], anchor_at(vbuf, shot), asend_sem.at[0], a_sem.at[1], t)
            return 0

        lax.fori_loop(0, HEADS, one, 0)

    def send_all(kind):
        def one(i, _):
            far = (2 + 3 * ((i // 3) * (i // 3 + 1) // 2)) % 4
            z = lax.rem(zh + far, 4)
            j = lax.rem(x + i, 3)
            h = z * 3 + j
            t = z * 4 + host_x(j, z, zl)
            if kind == 0:
                to_chip(q_ref.at[:, columns(h)], qbuf.at[chip], send_sem.at[0], q_sem, t)
            elif kind == 1:
                to_chip(k_ref.at[:, columns(h)], kbuf.at[chip, core], send_sem.at[1], k_sem.at[zh], t)
            else:
                to_chip(v_ref.at[:, columns(h)], vbuf.at[chip, core, :, pl.ds(0, HDIM)], send_sem.at[2], v_sem.at[zh], t)
            return 0

        lax.fori_loop(0, HEADS, one, 0)

    send_all(0)
    send_all(1)
    send_all(2)

    @pl.when(is_host)
    def _():
        @pl.when(core == 0)
        def _():
            drain(anchor_at(kbuf, shot), a_sem.at[0])
            drain(anchor_at(vbuf, shot), a_sem.at[1])
            remote(anchor_at(kbuf, shot), anchor_at(kbuf, shot), asend_sem.at[1], a_sem.at[2], partner).start()
            remote(anchor_at(vbuf, shot), anchor_at(vbuf, shot), asend_sem.at[1], a_sem.at[3], partner).start()
            other = y * 2 + 1 - zl
            drain(anchor_at(kbuf, other), a_sem.at[2])
            drain(anchor_at(vbuf, other), a_sem.at[3])

            def one(i, _):
                remote(pair_at(kbuf, y), pair_at(kbuf, y), asend_sem.at[2], a_sem.at[4], y_peer(i)).start()
                remote(pair_at(vbuf, y), pair_at(vbuf, y), asend_sem.at[2], a_sem.at[5], y_peer(i)).start()
                return 0

            lax.fori_loop(1, 8, one, 0)
            arrived = kbuf.at[pl.ds(0, 7), 0]
            drain(arrived, a_sem.at[4])
            drain(arrived, a_sem.at[5])
            all_k = kbuf.at[pl.ds(16, 4)]
            all_v = vbuf.at[pl.ds(16, 4), :, :, pl.ds(0, HDIM)]
            remote(all_k, all_k, asend_sem.at[3], f_sem.at[0], sibling).start()
            remote(all_v, all_v, asend_sem.at[3], f_sem.at[1], sibling).start()

        @pl.when(core == 1)
        def _():
            drain(kbuf.at[pl.ds(16, 4)], f_sem.at[0])
            drain(vbuf.at[pl.ds(16, 4), :, :, pl.ds(0, HDIM)], f_sem.at[1])

        def source(i):
            return lax.rem(zh + (2 + 3 * (i * (i + 1) // 2)) % 4, 4)

        def halves(buf, g, c):
            return buf.at[pl.ds(g * 4, 4), c, :, pl.ds(0, HDIM)]

        def take(buf, sem, fsem, g):
            drain(halves(buf, g, core), sem.at[g])
            remote(halves(buf, g, core), halves(buf, g, core), asend_sem.at[4], fsem.at[g], sibling).start()

        lane = lax.broadcasted_iota(jnp.int32, (8, GROUP), 1)
        mbuf[...] = jnp.full((QROWS, HDIM), DEAD, jnp.float32)

        def scores(slot, keys, bias):
            keys = keys.reshape(GROUP, HDIM)
            for r in range(0, QROWS, QB):
                rows = qbuf[r // ROWS : (r + QB) // ROWS].reshape(QB, HDIM)
                found = lax.dot_general(rows, keys, (((1,), (1,)), ((), ())), preferred_element_type=jnp.float32)
                found = found * SCALE + bias[:1]
                sbuf[slot, r : r + QB, :] = found
                top = mbuf[r : r + QB, :]
                for c in range(0, GROUP, HDIM):
                    top = jnp.maximum(top, found[:, c : c + HDIM])
                mbuf[r : r + QB, :] = top

        drain(qbuf, q_sem)
        limit = jnp.zeros((8, GROUP), jnp.int32)
        my_group = group_ref[shot]
        for t in range(SHOTS):
            seen = jnp.where(jnp.logical_and(group_ref[t] == my_group, shot != t), anch_ref[t], 0)
            limit = jnp.where(lane // ANCH == t, seen, limit)
        scores(4, kbuf[16:20], jnp.where(lane % ANCH < limit, 0.0, DEAD))
        live = len_ref[shot]

        def first(i, _):
            g = source(i)
            take(kbuf, k_sem, kf_sem, g)
            drain(halves(kbuf, g, 1 - core), kf_sem.at[g])
            scores(i, kbuf[pl.ds(g * 4, 4)], jnp.where(lane + g * GROUP < live, 0.0, DEAD))
            return 0

        lax.fori_loop(0, 4, first, 0)
        mbuf[...] = jnp.broadcast_to(jnp.max(mbuf[...], axis=1, keepdims=True), (QROWS, HDIM))

        def product(slot, rows, vals):
            weights = jnp.exp2(sbuf[slot, rows, :] - mbuf[rows, :1]).astype(jnp.bfloat16)
            return jnp.dot(weights, vals, preferred_element_type=jnp.float32)

        vals = vbuf[16:20].reshape(GROUP, 2 * HDIM)
        for r in range(0, QROWS, QB):
            acc[r : r + QB, :] = product(4, pl.ds(r, QB), vals)

        def second(i, _):
            g = source(i)
            take(vbuf, v_sem, vf_sem, g)
            drain(halves(vbuf, g, 1 - core), vf_sem.at[g])
            vals = vbuf[pl.ds(g * 4, 4)].reshape(GROUP, 2 * HDIM)
            for r in range(0, QROWS, QB):
                acc[r : r + QB, :] += product(i, pl.ds(r, QB), vals)
            return 0

        lax.fori_loop(0, 3, second, 0)
        g = source(3)
        take(vbuf, v_sem, vf_sem, g)
        drain(halves(vbuf, g, 1 - core), vf_sem.at[g])
        vals = vbuf[pl.ds(g * 4, 4)].reshape(GROUP, 2 * HDIM)
        for n in range(4):
            z = source(n)
            rows = pl.ds(pl.multiple_of(z * QB, QB), QB)
            done = acc[rows, :] + product(3, rows, vals)
            blended = done[:, :HDIM] / done[:, HDIM:]
            for k in range(4):
                t = z * 4 + k
                slots = (t * 2 + core) * ROWS + lax.broadcasted_iota(jnp.int32, (ROWS, HDIM), 0)
                piece = jnp.where(slots < live, blended[k * ROWS : (k + 1) * ROWS], 0.0)
                obuf[t] = piece.astype(jnp.bfloat16)
                to_chip(obuf.at[t], out_ref.at[:, columns(head)], os_sem, o_sem, t)

        drain(obuf.at[pl.ds(0, 15)], os_sem)

        drain(kbuf.at[pl.ds(0, CHIPS)], asend_sem.at[4])

        @pl.when(core == 0)
        def _():
            drain(kbuf.at[0, 0], asend_sem.at[1])
            drain(kbuf.at[pl.ds(0, 14), 0], asend_sem.at[2])
            drain(kbuf.at[pl.ds(0, 8)], asend_sem.at[3])

    @pl.when(seq == 0)
    def _():
        @pl.when(is_host)
        def _():
            drain(kbuf.at[pl.ds(0, 11), 0], asend_sem.at[0])

        @pl.when(jnp.logical_not(is_host))
        def _():
            drain(kbuf.at[pl.ds(0, 12), 0], asend_sem.at[0])

    for kind in range(3):
        @pl.when(is_host)
        def _():
            drain(q_ref.at[:, pl.ds(0, 11 * HDIM)], send_sem.at[kind])

        @pl.when(jnp.logical_not(is_host))
        def _():
            drain(q_ref, send_sem.at[kind])

    drain(out_ref, o_sem)


def local(queries, key_rows, values, shot_len, anchor_len, shot_group):
    whole = pl.BlockSpec(memory_space=pl.ANY)
    scalars = pl.BlockSpec(memory_space=pltpu.SMEM)
    dma = pltpu.SemaphoreType.DMA
    flat = (ROWS, HEADS * HDIM)
    out = pl.pallas_call(
        kernel,
        out_shape=jax.ShapeDtypeStruct(flat, jnp.bfloat16),
        in_specs=[scalars] * 3 + [whole] * 3,
        out_specs=whole,
        scratch_shapes=[
            pltpu.VMEM((CHIPS, ROWS, HDIM), jnp.bfloat16),
            pltpu.VMEM((20, 2, ROWS, HDIM), jnp.bfloat16),
            pltpu.VMEM((20, 2, ROWS, 2 * HDIM), jnp.bfloat16),
            pltpu.VMEM((CHIPS, ROWS, HDIM), jnp.bfloat16),
            pltpu.VMEM((5, QROWS, GROUP), jnp.float32),
            pltpu.VMEM((QROWS, HDIM), jnp.float32),
            pltpu.VMEM((QROWS, 2 * HDIM), jnp.float32),
            dma((3,)), dma, dma((4,)), dma((4,)), dma((4,)), dma((4,)),
            dma((6,)), dma((5,)), dma((2,)), dma, dma,
        ],
        compiler_params=pltpu.CompilerParams(
            collective_id=0, has_side_effects=True, vmem_limit_bytes=60 * 2**20
        ),
    )(
        shot_len, anchor_len, shot_group,
        queries.reshape(flat), key_rows.reshape(flat), values.reshape(flat),
    )
    return out.reshape(1, *flat)


def solution(mesh):
    spec = P("shot", "seq", None)
    return jax.shard_map(
        local, mesh=mesh, in_specs=(spec, spec, spec, P(), P(), P()), out_specs=spec, check_vma=False
    )
```

time: 637 us -> 92.6 us (0.15)
  waiting for transfers between devices: 292 us -> 0 us
  local copies, waits for them, and re-layouts: 112 us -> 1.77 us
  Pallas kernels: 0 us -> 90.6 us
  starting transfers between devices: 58.9 us -> 0 us
  blocking collectives: 53.1 us -> 0 us
  other arithmetic: 50.9 us -> 0 us
  matrix products: 48.6 us -> 0 us
  between operations: 13.7 us -> 0.01 us
    ppermute x7 -> x0, waiting for transfers between devices: 218 us -> none  [from_behind(): return lax.ppermute(block, axis, route)]
    pallas_call x0 -> x1, Pallas kernels: none -> 90.6 us  [local(): pl.pallas_call(kernel, out_shape=jax.ShapeDtypeStruct(flat, jnp.bfloat16)...]
    all_to_all x2 -> x0, blocking collectives: 53.1 us -> none  [the longest x1 33 us: local(): lax.all_to_all(finished, 'seq', split_axis=0, concat_axis=0, tiled=True)]
    all_gather x1 -> x0, waiting for transfers between devices: 48.6 us -> none  [local(): anchor_all = lax.all_gather(anchor_pair, 'shot', axis=1, tiled=True)]
    dot_general x36 -> x0, matrix products: 48.6 us -> none  [the longest x12 24.4 us: fill(): lax.dot_general(query_piece, key_piece, (((1,), (1,)), ((), ())), preferr...]
    all_to_all x2 -> x0, starting transfers between devices: 45 us -> none  [the longest x1 30.6 us: local(): lax.all_to_all(split_rows(queries), 'seq', split_axis=0, concat_axis=0, t...]
    while x66 -> x0, local copies, waits for them, and re-layouts: 38.1 us -> none  [the longest x6 34.2 us: one_rows(): lax.fori_loop(0, own_count, fill, jnp.full((query_block, shot_cap), -jnp....]
    all_to_all x2 -> x0, waiting for transfers between devices: 25.2 us -> none  [the longest x1 14.3 us: local(): lax.all_to_all(split_rows(values), 'seq', split_axis=0, concat_axis=0, ti...]
  transfers between devices with their start and end apart: 10 -> 0, of which waited for: 10 -> 0; matrix products, arithmetic and copies ran while one was open for 2% -> 0% of each run, Pallas kernels for 0% -> 0%
where the time goes in v1:
time: 92.6 us; the launch traced here: 92.4 us
  Pallas kernels  90.6 us (98%)
  local copies, waits for them, and re-layouts  1.77 us (2%)
    pallas_call x1, Pallas kernels, local(): pl.pallas_call(kernel, out_shape=jax.ShapeDtypeStruct(flat, jnp.bfloat16)...  90.6 us

profile of v1, /device:TPU:1, one launch (start us, length us, event | category | flops | bytes accessed | tf_op | source)
XLA Modules:
  0.0 92.4 jit_solution(14963820195126059662)
XLA Ops:
  0.0 90.6 %shard_map.64 = bf16[128,1536]{1,0:T(8,128)(2,1)} custom-call(s32[16]{0:T(128)} %len_ref.1, s32[16]{0:T(128)} %anch_ref.1, s32[16]{0:T(128)} %group_ref.1, bf16[128,1536]{1,0:T(8,128)(2,1)} %bitcast.5, bf16[128,1536]{1,0:T(8,128)(2,1)} %bitcast.6, bf16[128,1536]{1,0:T(8,128)(2,1)} %bitcast.7), custom_call_target="tpu_custom_call" | custom-call | tf_op jit(solution)/shard_map/pallas_call | solution.py:275
  90.6 1.8 %copy.8 = bf16[1,128,1536]{2,1,0:T(8,128)(2,1)} copy(bf16[1,128,1536]{2,1,0:T(8,128)(2,1)} %bitcast.4) | data formatting | bytes 786432

commit v2 on v1

v2 whole, which is shorter than its diff:
```python
import functools
import math

import jax
import jax.numpy as jnp
from jax import lax
from jax.experimental import pallas as pl
from jax.experimental.pallas import tpu as pltpu
from jax.sharding import PartitionSpec as P

MESH = pl.DeviceIdType.MESH
HEADS = 12
HDIM = 128
ANCH = 64
ROWS = 128
CHIPS = 16
SHOTS = 16
GROUP = 1024
QROWS = CHIPS * ROWS
QB = 512
DEAD = -1e30
AHEAD = 3
SCALE = math.log2(math.e) / math.sqrt(HDIM)


def kernel(
    len_ref, anch_ref, group_ref, q_ref, k_ref, v_ref, out_ref,
    qbuf, kbuf, vbuf, obuf, sbuf, mbuf,
    send_sem, q_sem, k_sem, v_sem, kf_sem, vf_sem, a_sem, asend_sem, f_sem, os_sem, o_sem,
):
    shot = lax.axis_index("shot")
    seq = lax.axis_index("seq")
    y, zl = shot // 2, shot % 2
    core, x, zh = seq % 2, (seq // 2) % 4, seq // 8
    here = x * 4 + zh
    is_host = x < 3
    head = zh * 3 + jnp.minimum(x, 2)

    vbuf[:, :, :, HDIM:] = jnp.ones((20, 2, ROWS, HDIM), jnp.bfloat16)

    sibling = (shot, seq + 1 - 2 * core)

    def mate(t):
        return (shot, (lax.rem(t, 4) * 4 + t // 4) * 2 + core)

    def y_peer(k):
        return (lax.rem(y + k, 8) * 2 + zl, seq)

    partner = (y * 2 + 1 - zl, seq)

    barrier = pltpu.get_barrier_semaphore()

    def greet(device):
        pl.semaphore_signal(barrier, inc=1, device_id=device, device_id_type=MESH)

    lax.fori_loop(1, CHIPS, lambda i, _: (greet(mate(lax.rem(here + i, CHIPS))), 0)[1], 0)
    lax.fori_loop(1, 8, lambda i, _: (greet(y_peer(i)), 0)[1], 0)
    greet(sibling)
    greet(partner)
    pl.semaphore_wait(barrier, CHIPS - 1 + 7 + 2)

    def remote(src, dst, ssem, rsem, device):
        return pltpu.make_async_remote_copy(
            src_ref=src, dst_ref=dst, send_sem=ssem, recv_sem=rsem,
            device_id=device, device_id_type=MESH,
        )

    def drain(ref, sem):
        pltpu.make_async_copy(ref, ref, sem).wait()

    def to_chip(src, dst, ssem, rsem, t):
        @pl.when(t == here)
        def _():
            pltpu.make_async_copy(src, dst, rsem).start()

        @pl.when(t != here)
        def _():
            remote(src, dst, ssem, rsem, mate(t)).start()

    def columns(h):
        return pl.ds(pl.multiple_of(h * HDIM, HDIM), HDIM)

    def anchor_at(buf, t):
        return buf.at[16 + t // 4, (t // 2) % 2, pl.ds(pl.multiple_of((t % 2) * ANCH, ANCH), ANCH), pl.ds(0, HDIM)]

    def pair_at(buf, yy):
        return buf.at[16 + yy // 2, yy % 2, :, pl.ds(0, HDIM)]

    @pl.when(seq == 0)
    def _():
        def one(h, _):
            t = lax.rem(h, 3) * 4 + h // 3
            to_chip(k_ref.at[pl.ds(0, ANCH), columns(h)], anchor_at(kbuf, shot), asend_sem.at[0], a_sem.at[0], t)
            to_chip(v_ref.at[pl.ds(0, ANCH), columns(h)], anchor_at(vbuf, shot), asend_sem.at[0], a_sem.at[1], t)
            return 0

        lax.fori_loop(0, HEADS, one, 0)

    def send(kind, turn):
        to_x = lax.rem(x + turn, 3)

        def one(n, _):
            z = lax.rem(zh + 2 + 3 * n, 4)
            h = z * 3 + to_x
            t = to_x * 4 + z
            if kind == 0:
                to_chip(q_ref.at[:, columns(h)], qbuf.at[here], send_sem.at[0, turn], q_sem, t)
            elif kind == 1:
                to_chip(k_ref.at[:, columns(h)], kbuf.at[here, core], send_sem.at[1, turn], k_sem.at[x], t)
            else:
                to_chip(v_ref.at[:, columns(h)], vbuf.at[here, core, :, pl.ds(0, HDIM)], send_sem.at[2, turn], v_sem.at[x], t)
            return 0

        lax.fori_loop(0, 4, one, 0)

    def sent(kind, turn):
        stayed = jnp.logical_and(turn == 0, is_host)

        @pl.when(jnp.logical_not(stayed))
        def _():
            drain(q_ref.at[:, pl.ds(0, 4 * HDIM)], send_sem.at[kind, turn])

        @pl.when(stayed)
        def _():
            drain(q_ref.at[:, pl.ds(0, 3 * HDIM)], send_sem.at[kind, turn])

    def send_next(n):
        sent((n - AHEAD) // 3, (n - AHEAD) % 3)
        send(n // 3, n % 3)

    for n in range(AHEAD):
        send(n // 3, n % 3)

    @pl.when(jnp.logical_not(is_host))
    def _():
        for n in range(AHEAD, 9):
            send_next(n)

    @pl.when(is_host)
    def _():
        all_k = kbuf.at[pl.ds(16, 4)]
        all_v = vbuf.at[pl.ds(16, 4), :, :, pl.ds(0, HDIM)]

        def anchors_to_partner():
            drain(anchor_at(kbuf, shot), a_sem.at[0])
            drain(anchor_at(vbuf, shot), a_sem.at[1])
            remote(anchor_at(kbuf, shot), anchor_at(kbuf, shot), asend_sem.at[1], a_sem.at[2], partner).start()
            remote(anchor_at(vbuf, shot), anchor_at(vbuf, shot), asend_sem.at[1], a_sem.at[3], partner).start()

        def anchors_to_peers():
            other = y * 2 + 1 - zl
            drain(anchor_at(kbuf, other), a_sem.at[2])
            drain(anchor_at(vbuf, other), a_sem.at[3])

            def one(i, _):
                remote(pair_at(kbuf, y), pair_at(kbuf, y), asend_sem.at[2], a_sem.at[4], y_peer(i)).start()
                remote(pair_at(vbuf, y), pair_at(vbuf, y), asend_sem.at[2], a_sem.at[5], y_peer(i)).start()
                return 0

            lax.fori_loop(1, 8, one, 0)

        def anchors_to_sibling():
            arrived = kbuf.at[pl.ds(0, 7), 0]
            drain(arrived, a_sem.at[4])
            drain(arrived, a_sem.at[5])
            remote(all_k, all_k, asend_sem.at[3], f_sem.at[0], sibling).start()
            remote(all_v, all_v, asend_sem.at[3], f_sem.at[1], sibling).start()

        @pl.when(core == 0)
        def _():
            anchors_to_partner()

        send_next(3)

        @pl.when(core == 0)
        def _():
            anchors_to_peers()

        send_next(4)
        send_next(5)

        def source(i):
            return lax.rem(x + 4 - i, 4)

        def halves(buf, g, c):
            return buf.at[pl.ds(g * 4, 4), c, :, pl.ds(0, HDIM)]

        def take(buf, sem, fsem, g):
            drain(halves(buf, g, core), sem.at[g])
            remote(halves(buf, g, core), halves(buf, g, core), asend_sem.at[4], fsem.at[g], sibling).start()

        lane = lax.broadcasted_iota(jnp.int32, (8, GROUP), 1)
        mbuf[...] = jnp.full((QROWS, HDIM), DEAD, jnp.float32)

        def scores(slot, keys, bias):
            keys = keys.reshape(GROUP, HDIM)
            for r in range(0, QROWS, QB):
                rows = qbuf[r // ROWS : (r + QB) // ROWS].reshape(QB, HDIM)
                found = lax.dot_general(rows, keys, (((1,), (1,)), ((), ())), preferred_element_type=jnp.float32)
                found = found * SCALE + bias[:1]
                sbuf[slot, r : r + QB, :] = found
                top = mbuf[r : r + QB, :]
                for c in range(0, GROUP, HDIM):
                    top = jnp.maximum(top, found[:, c : c + HDIM])
                mbuf[r : r + QB, :] = top

        drain(qbuf, q_sem)

        live = len_ref[shot]

        def first(i, _):
            g = source(i)

            @pl.when(i == 0)
            def _():
                send_next(6)

            @pl.when(i == 1)
            def _():
                send_next(7)

            @pl.when(i == 2)
            def _():
                send_next(8)

            take(kbuf, k_sem, kf_sem, g)

            @pl.when(jnp.logical_and(core == 0, i == 3))
            def _():
                anchors_to_sibling()

            drain(halves(kbuf, g, 1 - core), kf_sem.at[g])
            slot = ((lane // (2 * ROWS)) * 4 + g) * (2 * ROWS) + lane % (2 * ROWS)
            scores(i, kbuf[pl.ds(g * 4, 4)], jnp.where(slot < live, 0.0, DEAD))
            return 0

        lax.fori_loop(0, 4, first, 0)
        limit = jnp.zeros((8, GROUP), jnp.int32)
        my_group = group_ref[shot]
        for t in range(SHOTS):
            seen = jnp.where(jnp.logical_and(group_ref[t] == my_group, shot != t), anch_ref[t], 0)
            limit = jnp.where(lane // ANCH == t, seen, limit)

        @pl.when(core == 1)
        def _():
            drain(all_k, f_sem.at[0])
            drain(all_v, f_sem.at[1])

        scores(4, kbuf[16:20], jnp.where(lane % ANCH < limit, 0.0, DEAD))
        mbuf[...] = jnp.broadcast_to(jnp.max(mbuf[...], axis=1, keepdims=True), (QROWS, HDIM))

        lax.fori_loop(0, 4, lambda i, _: (take(vbuf, v_sem, vf_sem, source(i)), 0)[1], 0)
        lax.fori_loop(0, 4, lambda i, _: (drain(halves(vbuf, i, 1 - core), vf_sem.at[i]), 0)[1], 0)

        def product(slot, rows, first):
            weights = jnp.exp2(sbuf[slot, rows, :] - mbuf[rows, :1]).astype(jnp.bfloat16)
            vals = vbuf[pl.ds(first, 4)].reshape(GROUP, 2 * HDIM)
            return jnp.dot(weights, vals, preferred_element_type=jnp.float32)

        for n in range(4):
            to_x = lax.rem(x + n + 1, 4)
            rows = pl.ds(pl.multiple_of(to_x * QB, QB), QB)
            done = product(4, rows, 16)
            for i in range(4):
                done += product(i, rows, source(i) * 4)
            blended = done[:, :HDIM] / done[:, HDIM:]
            for k in range(4):
                t = to_x * 4 + k
                slots = ((k * 4 + to_x) * 2 + core) * ROWS + lax.broadcasted_iota(jnp.int32, (ROWS, HDIM), 0)
                piece = jnp.where(slots < live, blended[k * ROWS : (k + 1) * ROWS], 0.0)
                obuf[t] = piece.astype(jnp.bfloat16)
                to_chip(obuf.at[t], out_ref.at[:, columns(head)], os_sem, o_sem, t)

        drain(obuf.at[pl.ds(0, 15)], os_sem)

        drain(kbuf.at[pl.ds(0, CHIPS)], asend_sem.at[4])

        @pl.when(core == 0)
        def _():
            drain(kbuf.at[0, 0], asend_sem.at[1])
            drain(kbuf.at[pl.ds(0, 14), 0], asend_sem.at[2])
            drain(kbuf.at[pl.ds(0, 8)], asend_sem.at[3])

    @pl.when(seq == 0)
    def _():
        @pl.when(is_host)
        def _():
            drain(kbuf.at[pl.ds(0, 11), 0], asend_sem.at[0])

        @pl.when(jnp.logical_not(is_host))
        def _():
            drain(kbuf.at[pl.ds(0, 12), 0], asend_sem.at[0])

    for n in range(9 - AHEAD, 9):
        sent(n // 3, n % 3)
    drain(out_ref, o_sem)


def local(queries, key_rows, values, shot_len, anchor_len, shot_group):
    whole = pl.BlockSpec(memory_space=pl.ANY)
    scalars = pl.BlockSpec(memory_space=pltpu.SMEM)
    dma = pltpu.SemaphoreType.DMA
    flat = (ROWS, HEADS * HDIM)
    out = pl.pallas_call(
        kernel,
        out_shape=jax.ShapeDtypeStruct(flat, jnp.bfloat16),
        in_specs=[scalars] * 3 + [whole] * 3,
        out_specs=whole,
        scratch_shapes=[
            pltpu.VMEM((CHIPS, ROWS, HDIM), jnp.bfloat16),
            pltpu.VMEM((20, 2, ROWS, HDIM), jnp.bfloat16),
            pltpu.VMEM((20, 2, ROWS, 2 * HDIM), jnp.bfloat16),
            pltpu.VMEM((CHIPS, ROWS, HDIM), jnp.bfloat16),
            pltpu.VMEM((5, QROWS, GROUP), jnp.float32),
            pltpu.VMEM((QROWS, HDIM), jnp.float32),
            dma((3, 3)), dma, dma((4,)), dma((4,)), dma((4,)), dma((4,)),
            dma((6,)), dma((5,)), dma((2,)), dma, dma,
        ],
        compiler_params=pltpu.CompilerParams(
            collective_id=0, has_side_effects=True, vmem_limit_bytes=60 * 2**20
        ),
    )(
        shot_len, anchor_len, shot_group,
        queries.reshape(flat), key_rows.reshape(flat), values.reshape(flat),
    )
    return out.reshape(1, *flat)


def solution(mesh):
    spec = P("shot", "seq", None)
    return jax.shard_map(
        local, mesh=mesh, in_specs=(spec, spec, spec, P(), P(), P()), out_specs=spec, check_vma=False
    )
```

time: 92.6 us -> 71.8 us (0.78)
  Pallas kernels: 90.6 us -> 69.8 us
    pallas_call x1, Pallas kernels: 90.6 us -> 69.8 us  [local(): pl.pallas_call(kernel, out_shape=jax.ShapeDtypeStruct(flat, jnp.bfloat16)...]
where the time goes in v2:
time: 71.8 us; the launch traced here: 71.6 us
  Pallas kernels  69.8 us (97%)
  local copies, waits for them, and re-layouts  1.77 us (2%)
    pallas_call x1, Pallas kernels, local(): pl.pallas_call(kernel, out_shape=jax.ShapeDtypeStruct(flat, jnp.bfloat16)...  69.8 us
    unnamed x1, local copies, waits for them, and re-layouts  1.77 us

profile of v2, /device:TPU:1, one launch (start us, length us, event | category | flops | bytes accessed | tf_op | source)
XLA Modules:
  0.0 71.6 jit_solution(5390927192166817843)
XLA Ops:
  0.0 69.8 %shard_map.64 = bf16[128,1536]{1,0:T(8,128)(2,1)} custom-call(s32[16]{0:T(128)} %len_ref.1, s32[16]{0:T(128)} %anch_ref.1, s32[16]{0:T(128)} %group_ref.1, bf16[128,1536]{1,0:T(8,128)(2,1)} %bitcast.5, bf16[128,1536]{1,0:T(8,128)(2,1)} %bitcast.6, bf16[128,1536]{1,0:T(8,128)(2,1)} %bitcast.7), custom_call_target="tpu_custom_call" | custom-call | tf_op jit(solution)/shard_map/pallas_call | solution.py:304
  69.8 1.8 %copy.8 = bf16[1,128,1536]{2,1,0:T(8,128)(2,1)} copy(bf16[1,128,1536]{2,1,0:T(8,128)(2,1)} %bitcast.4) | data formatting | bytes 786432

commit v3 on v2

--- a/solution.py
+++ b/solution.py
@@ -15,7 +15,7 @@
 ROWS = 128
 CHIPS = 16
 SHOTS = 16
-GROUP = 1024
+GROUP = 512
 QROWS = CHIPS * ROWS
 QB = 512
 DEAD = -1e30
@@ -25,7 +25,7 @@
 
 def kernel(
     len_ref, anch_ref, group_ref, q_ref, k_ref, v_ref, out_ref,
-    qbuf, kbuf, vbuf, obuf, sbuf, mbuf,
+    qbuf, kbuf, vbuf, obuf, sbuf, mbuf, first_vals,
     send_sem, q_sem, k_sem, v_sem, kf_sem, vf_sem, a_sem, asend_sem, f_sem, os_sem, o_sem,
 ):
     shot = lax.axis_index("shot")
@@ -36,7 +36,7 @@
     is_host = x < 3
     head = zh * 3 + jnp.minimum(x, 2)
 
-    vbuf[:, :, :, HDIM:] = jnp.ones((20, 2, ROWS, HDIM), jnp.bfloat16)
+    vbuf[:, :, :, HDIM:] = jnp.ones((2, 20, ROWS, HDIM), jnp.bfloat16)
 
     sibling = (shot, seq + 1 - 2 * core)
 
@@ -81,20 +81,22 @@
         return pl.ds(pl.multiple_of(h * HDIM, HDIM), HDIM)
 
     def anchor_at(buf, t):
-        return buf.at[16 + t // 4, (t // 2) % 2, pl.ds(pl.multiple_of((t % 2) * ANCH, ANCH), ANCH), pl.ds(0, HDIM)]
+        return buf.at[(t // 2) % 2, 16 + t // 4, pl.ds(pl.multiple_of((t % 2) * ANCH, ANCH), ANCH), pl.ds(0, HDIM)]
 
     def pair_at(buf, yy):
-        return buf.at[16 + yy // 2, yy % 2, :, pl.ds(0, HDIM)]
+        return buf.at[yy % 2, 16 + yy // 2, :, pl.ds(0, HDIM)]
+
+    def anchors_out(src, buf):
+        def one(h, _):
+            to_chip(src.at[pl.ds(0, ANCH), columns(h)], anchor_at(buf, shot), asend_sem.at[0], a_sem.at[0], lax.rem(h, 3) * 4 + h // 3)
+            return 0
+
+        lax.fori_loop(0, HEADS, one, 0)
 
     @pl.when(seq == 0)
     def _():
-        def one(h, _):
-            t = lax.rem(h, 3) * 4 + h // 3
-            to_chip(k_ref.at[pl.ds(0, ANCH), columns(h)], anchor_at(kbuf, shot), asend_sem.at[0], a_sem.at[0], t)
-            to_chip(v_ref.at[pl.ds(0, ANCH), columns(h)], anchor_at(vbuf, shot), asend_sem.at[0], a_sem.at[1], t)
-            return 0
-
-        lax.fori_loop(0, HEADS, one, 0)
+        remote(v_ref.at[pl.ds(0, ANCH)], first_vals, asend_sem.at[5], a_sem.at[3], sibling).start()
+        anchors_out(k_ref, kbuf)
 
     def send(kind, turn):
         to_x = lax.rem(x + turn, 3)
@@ -106,9 +108,9 @@
             if kind == 0:
                 to_chip(q_ref.at[:, columns(h)], qbuf.at[here], send_sem.at[0, turn], q_sem, t)
             elif kind == 1:
-                to_chip(k_ref.at[:, columns(h)], kbuf.at[here, core], send_sem.at[1, turn], k_sem.at[x], t)
+                to_chip(k_ref.at[:, columns(h)], kbuf.at[core, here], send_sem.at[1, turn], k_sem.at[x], t)
             else:
-                to_chip(v_ref.at[:, columns(h)], vbuf.at[here, core, :, pl.ds(0, HDIM)], send_sem.at[2, turn], v_sem.at[x], t)
+                to_chip(v_ref.at[:, columns(h)], vbuf.at[core, here, :, pl.ds(0, HDIM)], send_sem.at[2, turn], v_sem.at[x], t)
             return 0
 
         lax.fori_loop(0, 4, one, 0)
@@ -131,6 +133,11 @@
     for n in range(AHEAD):
         send(n // 3, n % 3)
 
+    @pl.when(seq == 1)
+    def _():
+        drain(first_vals, a_sem.at[3])
+        anchors_out(first_vals, vbuf)
+
     @pl.when(jnp.logical_not(is_host))
     def _():
         for n in range(AHEAD, 9):
@@ -138,44 +145,38 @@
 
     @pl.when(is_host)
     def _():
-        all_k = kbuf.at[pl.ds(16, 4)]
-        all_v = vbuf.at[pl.ds(16, 4), :, :, pl.ds(0, HDIM)]
-
-        def anchors_to_partner():
-            drain(anchor_at(kbuf, shot), a_sem.at[0])
-            drain(anchor_at(vbuf, shot), a_sem.at[1])
-            remote(anchor_at(kbuf, shot), anchor_at(kbuf, shot), asend_sem.at[1], a_sem.at[2], partner).start()
-            remote(anchor_at(vbuf, shot), anchor_at(vbuf, shot), asend_sem.at[1], a_sem.at[3], partner).start()
-
-        def anchors_to_peers():
-            other = y * 2 + 1 - zl
-            drain(anchor_at(kbuf, other), a_sem.at[2])
-            drain(anchor_at(vbuf, other), a_sem.at[3])
+        all_k = kbuf.at[:, pl.ds(16, 4)]
+        all_v = vbuf.at[:, pl.ds(16, 4), :, pl.ds(0, HDIM)]
+
+        def anchors_to_partner(buf):
+            drain(anchor_at(buf, shot), a_sem.at[0])
+            remote(anchor_at(buf, shot), anchor_at(buf, shot), asend_sem.at[1], a_sem.at[1], partner).start()
+
+        def anchors_to_peers(buf):
+            drain(anchor_at(buf, y * 2 + 1 - zl), a_sem.at[1])
 
             def one(i, _):
-                remote(pair_at(kbuf, y), pair_at(kbuf, y), asend_sem.at[2], a_sem.at[4], y_peer(i)).start()
-                remote(pair_at(vbuf, y), pair_at(vbuf, y), asend_sem.at[2], a_sem.at[5], y_peer(i)).start()
+                remote(pair_at(buf, y), pair_at(buf, y), asend_sem.at[2], a_sem.at[2], y_peer(i)).start()
                 return 0
 
             lax.fori_loop(1, 8, one, 0)
 
-        def anchors_to_sibling():
-            arrived = kbuf.at[pl.ds(0, 7), 0]
-            drain(arrived, a_sem.at[4])
-            drain(arrived, a_sem.at[5])
-            remote(all_k, all_k, asend_sem.at[3], f_sem.at[0], sibling).start()
-            remote(all_v, all_v, asend_sem.at[3], f_sem.at[1], sibling).start()
-
-        @pl.when(core == 0)
-        def _():
-            anchors_to_partner()
-
+        def anchors_to_sibling(part):
+            drain(kbuf.at[0, pl.ds(0, 7)], a_sem.at[2])
+            remote(part, part, asend_sem.at[3], f_sem, sibling).start()
+
+        def by_core(step, keys, vals):
+            @pl.when(core == 0)
+            def _():
+                step(keys)
+
+            @pl.when(core == 1)
+            def _():
+                step(vals)
+
+        by_core(anchors_to_partner, kbuf, vbuf)
         send_next(3)
-
-        @pl.when(core == 0)
-        def _():
-            anchors_to_peers()
-
+        by_core(anchors_to_peers, kbuf, vbuf)
         send_next(4)
         send_next(5)
 
@@ -183,7 +184,7 @@
             return lax.rem(x + 4 - i, 4)
 
         def halves(buf, g, c):
-            return buf.at[pl.ds(g * 4, 4), c, :, pl.ds(0, HDIM)]
+            return buf.at[c, pl.ds(g * 4, 4), :, pl.ds(0, HDIM)]
 
         def take(buf, sem, fsem, g):
             drain(halves(buf, g, core), sem.at[g])
@@ -225,44 +226,57 @@
 
             take(kbuf, k_sem, kf_sem, g)
 
-            @pl.when(jnp.logical_and(core == 0, i == 3))
-            def _():
-                anchors_to_sibling()
-
+            @pl.when(i == 3)
+            def _():
+                by_core(anchors_to_sibling, all_k, all_v)
+
+
+            def half(c):
+                slot = ((lane // ROWS) * 4 + g) * (2 * ROWS) + c * ROWS + lane % ROWS
+                scores(2 * i + jnp.where(c == core, 0, 1), kbuf[c, pl.ds(g * 4, 4)], jnp.where(slot < live, 0.0, DEAD))
+
+            half(core)
             drain(halves(kbuf, g, 1 - core), kf_sem.at[g])
-            slot = ((lane // (2 * ROWS)) * 4 + g) * (2 * ROWS) + lane % (2 * ROWS)
-            scores(i, kbuf[pl.ds(g * 4, 4)], jnp.where(slot < live, 0.0, DEAD))
+            half(1 - core)
             return 0
 
         lax.fori_loop(0, 4, first, 0)
-        limit = jnp.zeros((8, GROUP), jnp.int32)
         my_group = group_ref[shot]
-        for t in range(SHOTS):
-            seen = jnp.where(jnp.logical_and(group_ref[t] == my_group, shot != t), anch_ref[t], 0)
-            limit = jnp.where(lane // ANCH == t, seen, limit)
 
         @pl.when(core == 1)
         def _():
-            drain(all_k, f_sem.at[0])
-            drain(all_v, f_sem.at[1])
-
-        scores(4, kbuf[16:20], jnp.where(lane % ANCH < limit, 0.0, DEAD))
+            drain(all_k, f_sem)
+
+        for c in range(2):
+            limit = jnp.zeros((8, GROUP), jnp.int32)
+            for n in range(SHOTS // 2):
+                t = (n // 2) * 4 + c * 2 + n % 2
+                seen = jnp.where(jnp.logical_and(group_ref[t] == my_group, shot != t), anch_ref[t], 0)
+                limit = jnp.where(lane // ANCH == n, seen, limit)
+            scores(8 + c, kbuf[c, 16:20], jnp.where(lane % ANCH < limit, 0.0, DEAD))
         mbuf[...] = jnp.broadcast_to(jnp.max(mbuf[...], axis=1, keepdims=True), (QROWS, HDIM))
 
+        @pl.when(core == 0)
+        def _():
+            drain(all_v, f_sem)
+
         lax.fori_loop(0, 4, lambda i, _: (take(vbuf, v_sem, vf_sem, source(i)), 0)[1], 0)
-        lax.fori_loop(0, 4, lambda i, _: (drain(halves(vbuf, i, 1 - core), vf_sem.at[i]), 0)[1], 0)
-
-        def product(slot, rows, first):
+
+        def product(slot, rows, c, first):
             weights = jnp.exp2(sbuf[slot, rows, :] - mbuf[rows, :1]).astype(jnp.bfloat16)
-            vals = vbuf[pl.ds(first, 4)].reshape(GROUP, 2 * HDIM)
+            vals = vbuf[c, pl.ds(first, 4)].reshape(GROUP, 2 * HDIM)
             return jnp.dot(weights, vals, preferred_element_type=jnp.float32)
 
         for n in range(4):
             to_x = lax.rem(x + n + 1, 4)
             rows = pl.ds(pl.multiple_of(to_x * QB, QB), QB)
-            done = product(4, rows, 16)
+            done = product(8, rows, 0, 16) + product(9, rows, 1, 16)
             for i in range(4):
-                done += product(i, rows, source(i) * 4)
+                done += product(2 * i, rows, core, source(i) * 4)
+            if n == 0:
+                lax.fori_loop(0, 4, lambda i, _: (drain(halves(vbuf, i, 1 - core), vf_sem.at[i]), 0)[1], 0)
+            for i in range(4):
+                done += product(2 * i + 1, rows, 1 - core, source(i) * 4)
             blended = done[:, :HDIM] / done[:, HDIM:]
             for k in range(4):
                 t = to_x * 4 + k
@@ -273,23 +287,19 @@
 
         drain(obuf.at[pl.ds(0, 15)], os_sem)
 
-        drain(kbuf.at[pl.ds(0, CHIPS)], asend_sem.at[4])
-
-        @pl.when(core == 0)
-        def _():
-            drain(kbuf.at[0, 0], asend_sem.at[1])
-            drain(kbuf.at[pl.ds(0, 14), 0], asend_sem.at[2])
-            drain(kbuf.at[pl.ds(0, 8)], asend_sem.at[3])
+        drain(kbuf.at[:, pl.ds(0, CHIPS)], asend_sem.at[4])
+
+        drain(anchor_at(kbuf, 0), asend_sem.at[1])
+        drain(kbuf.at[0, pl.ds(0, 7)], asend_sem.at[2])
+        drain(all_k, asend_sem.at[3])
+
+    @pl.when(seq < 2)
+    def _():
+        drain(kbuf.at[0, pl.ds(0, HEADS - 1), pl.ds(0, ANCH)], asend_sem.at[0])
 
     @pl.when(seq == 0)
     def _():
-        @pl.when(is_host)
-        def _():
-            drain(kbuf.at[pl.ds(0, 11), 0], asend_sem.at[0])
-
-        @pl.when(jnp.logical_not(is_host))
-        def _():
-            drain(kbuf.at[pl.ds(0, 12), 0], asend_sem.at[0])
+        drain(first_vals, asend_sem.at[5])
 
     for n in range(9 - AHEAD, 9):
         sent(n // 3, n % 3)
@@ -308,13 +318,14 @@
         out_specs=whole,
         scratch_shapes=[
             pltpu.VMEM((CHIPS, ROWS, HDIM), jnp.bfloat16),
-            pltpu.VMEM((20, 2, ROWS, HDIM), jnp.bfloat16),
-            pltpu.VMEM((20, 2, ROWS, 2 * HDIM), jnp.bfloat16),
+            pltpu.VMEM((2, 20, ROWS, HDIM), jnp.bfloat16),
+            pltpu.VMEM((2, 20, ROWS, 2 * HDIM), jnp.bfloat16),
             pltpu.VMEM((CHIPS, ROWS, HDIM), jnp.bfloat16),
-            pltpu.VMEM((5, QROWS, GROUP), jnp.float32),
+            pltpu.VMEM((10, QROWS, GROUP), jnp.float32),
             pltpu.VMEM((QROWS, HDIM), jnp.float32),
+            pltpu.VMEM((ANCH, HEADS * HDIM), jnp.bfloat16),
             dma((3, 3)), dma, dma((4,)), dma((4,)), dma((4,)), dma((4,)),
-            dma((6,)), dma((5,)), dma((2,)), dma, dma,
+            dma((4,)), dma((6,)), dma, dma, dma,
         ],
         compiler_params=pltpu.CompilerParams(
             collective_id=0, has_side_effects=True, vmem_limit_bytes=60 * 2**20

time: 71.8 us -> 67.5 us (0.940)
  the two profiles are of different devices: /device:TPU:1 before, /device:TPU:66 now
where the time goes in v3:
time: 67.5 us; the launch traced here: 67.3 us
  Pallas kernels  65.5 us (97%)
  local copies, waits for them, and re-layouts  1.77 us (3%)
    pallas_call x1, Pallas kernels, local(): pl.pallas_call(kernel, out_shape=jax.ShapeDtypeStruct(flat, jnp.bfloat16)...  65.5 us
    unnamed x1, local copies, waits for them, and re-layouts  1.77 us

profile of v3, /device:TPU:66, one launch (start us, length us, event | category | flops | bytes accessed | tf_op | source)
XLA Modules:
  0.0 67.3 jit_solution(528014708822790478)
XLA Ops:
  0.0 65.5 %shard_map.64 = bf16[128,1536]{1,0:T(8,128)(2,1)} custom-call(s32[16]{0:T(128)} %len_ref.1, s32[16]{0:T(128)} %anch_ref.1, s32[16]{0:T(128)} %group_ref.1, bf16[128,1536]{1,0:T(8,128)(2,1)} %bitcast.5, bf16[128,1536]{1,0:T(8,128)(2,1)} %bitcast.6, bf16[128,1536]{1,0:T(8,128)(2,1)} %bitcast.7), custom_call_target="tpu_custom_call" | custom-call | tf_op jit(solution)/shard_map/pallas_call | solution.py:314
  65.6 1.8 %copy.8 = bf16[1,128,1536]{2,1,0:T(8,128)(2,1)} copy(bf16[1,128,1536]{2,1,0:T(8,128)(2,1)} %bitcast.4) | data formatting | bytes 786432

commit v4 on v3

--- a/solution.py
+++ b/solution.py
@@ -18,6 +18,7 @@
 GROUP = 512
 QROWS = CHIPS * ROWS
 QB = 512
+QB2 = 256
 DEAD = -1e30
 AHEAD = 3
 SCALE = math.log2(math.e) / math.sqrt(HDIM)
@@ -267,9 +268,9 @@
             vals = vbuf[c, pl.ds(first, 4)].reshape(GROUP, 2 * HDIM)
             return jnp.dot(weights, vals, preferred_element_type=jnp.float32)
 
-        for n in range(4):
-            to_x = lax.rem(x + n + 1, 4)
-            rows = pl.ds(pl.multiple_of(to_x * QB, QB), QB)
+        for n in range(QROWS // QB2):
+            to_x = lax.rem(x + n // 2 + 1, 4)
+            rows = pl.ds(pl.multiple_of(to_x * QB + n % 2 * QB2, QB2), QB2)
             done = product(8, rows, 0, 16) + product(9, rows, 1, 16)
             for i in range(4):
                 done += product(2 * i, rows, core, source(i) * 4)
@@ -278,9 +279,9 @@
             for i in range(4):
                 done += product(2 * i + 1, rows, 1 - core, source(i) * 4)
             blended = done[:, :HDIM] / done[:, HDIM:]
-            for k in range(4):
-                t = to_x * 4 + k
-                slots = ((k * 4 + to_x) * 2 + core) * ROWS + lax.broadcasted_iota(jnp.int32, (ROWS, HDIM), 0)
+            for k in range(2):
+                t = to_x * 4 + n % 2 * 2 + k
+                slots = (((n % 2 * 2 + k) * 4 + to_x) * 2 + core) * ROWS + lax.broadcasted_iota(jnp.int32, (ROWS, HDIM), 0)
                 piece = jnp.where(slots < live, blended[k * ROWS : (k + 1) * ROWS], 0.0)
                 obuf[t] = piece.astype(jnp.bfloat16)
                 to_chip(obuf.at[t], out_ref.at[:, columns(head)], os_sem, o_sem, t)

time: 67.5 us -> 66.7 us (0.988)
  the two profiles are of different devices: /device:TPU:66 before, /device:TPU:1 now
where the time goes in v4:
time: 66.7 us; the launch traced here: 65.8 us
  Pallas kernels  64.1 us (96%)
  local copies, waits for them, and re-layouts  1.77 us (3%)
    pallas_call x1, Pallas kernels, local(): pl.pallas_call(kernel, out_shape=jax.ShapeDtypeStruct(flat, jnp.bfloat16)...  64.1 us
    unnamed x1, local copies, waits for them, and re-layouts  1.77 us

profile of v4, /device:TPU:1, one launch (start us, length us, event | category | flops | bytes accessed | tf_op | source)
XLA Modules:
  0.0 65.8 jit_solution(1095039437062666699)
XLA Ops:
  0.0 64.1 %shard_map.64 = bf16[128,1536]{1,0:T(8,128)(2,1)} custom-call(s32[16]{0:T(128)} %len_ref.1, s32[16]{0:T(128)} %anch_ref.1, s32[16]{0:T(128)} %group_ref.1, bf16[128,1536]{1,0:T(8,128)(2,1)} %bitcast.5, bf16[128,1536]{1,0:T(8,128)(2,1)} %bitcast.6, bf16[128,1536]{1,0:T(8,128)(2,1)} %bitcast.7), custom_call_target="tpu_custom_call" | custom-call | tf_op jit(solution)/shard_map/pallas_call | solution.py:315
  64.1 1.8 %copy.8 = bf16[1,128,1536]{2,1,0:T(8,128)(2,1)} copy(bf16[1,128,1536]{2,1,0:T(8,128)(2,1)} %bitcast.4) | data formatting | bytes 786432
